TPU v7x, 256 devices: a whole 4x4x8 slice. The times are simulated.
256 devices in a mesh: gx: 64 (over y, z_lo, x), gy: 4 (over z_hi, core).
Axes of the slice: x: 4, y: 4, z: 8 (z_hi: 2, z_lo: 4; z = z_hi * 4 + z_lo), core: 2. Of those that a mesh axis runs over, the one named last changes fastest.
Arguments:
- tracers: float32 [768, 256, 2, 128], P('gx', 'gy'), may hold values from -6 to 6
- weights: float32 [768, 256, 48], P('gx', 'gy'), may hold values from 0 to 0.5
- offsets: int32 [768, 256, 4], P('gx', 'gy'), may hold values from -2 to 1
- owner: int32 [2, 64], replicated, may hold values from 0 to 63, as said below
- codes: int32 [2, 64], replicated, may hold values from 0 to 3
Outputs:
- updated: float32 [768, 256, 2, 128], P('gx', 'gy')
Inputs may be any that keep to these rules, and one draw needn't show every extreme that they name: owner[0, b] names the column block whose first three rows are glued below block b, owner[1, b] the one whose last three rows are glued above it; each row of owner is a permutation of the 64 blocks, so every block's edge rows are glued to exactly one block on each side. `codes`: bit 0 reverses the glued rows along the columns, bit 1 reverses their order.
All inputs are finite; a program needn't handle non-finite values.
Results may differ from a plain program's by a relative error of at most 0.0003.
Values sent between devices are 32-bit elements; how exact they have to be, the bound alone decides.
A program may use at most 128 MiB of HBM per device.

v0:
```python
import jax
import jax.numpy as jnp
from jax import lax
from jax.sharding import PartitionSpec as P


def padded(cells, sides, width):
    for axis, dim in sides:
        count = lax.axis_size(axis)
        head = lax.slice_in_dim(cells, 0, width, axis=dim)
        tail = lax.slice_in_dim(cells, cells.shape[dim] - width, cells.shape[dim], axis=dim)
        cells = jnp.concatenate(
            [
                lax.ppermute(tail, axis, [(i, (i + 1) % count) for i in range(count)]),
                cells,
                lax.ppermute(head, axis, [((i + 1) % count, i) for i in range(count)]),
            ],
            axis=dim,
        )
    return cells


def sent_together(arrays, axis, dim, along):
    ends, at = ([], 0)
    for a in arrays[:-1]:
        at += a.shape[along]
        ends.append(at)
    both = jnp.concatenate(arrays, axis=along)
    return tuple(jnp.split(lax.all_gather(both, axis, axis=dim, tiled=True), ends, axis=along))


def moment_list(extended):
    centre = extended[1:-1, 1:-1]
    east_side = extended[2:, 1:-1]
    west_side = extended[:-2, 1:-1]
    north_side = extended[1:-1, 2:]
    south_side = extended[1:-1, :-2]
    slope_east = 0.5 * (east_side - west_side)
    slope_north = 0.5 * (north_side - south_side)
    curve_east = 0.5 * (east_side - 2.0 * centre + west_side)
    curve_north = 0.5 * (north_side - 2.0 * centre + south_side)
    twist_both = 0.25 * (
        extended[2:, 2:] - extended[2:, :-2] - extended[:-2, 2:] + extended[:-2, :-2]
    )
    return [centre, slope_east, slope_north, curve_east, curve_north, twist_both]


def remap_block(extended, weights, offsets):
    cols_out, rows_out = (weights.shape[0], weights.shape[1])
    levels = offsets.shape[2] // 2
    tracer_count = extended.shape[3]
    moments = moment_list(extended)
    results = []
    for level_index in range(levels):
        shift_col = offsets[:, :, 2 * level_index]
        shift_row = offsets[:, :, 2 * level_index + 1]
        summed = jnp.zeros((cols_out, rows_out, tracer_count), jnp.float32)
        for total_col in range(-2, 3):
            for total_row in range(-2, 3):
                combined = jnp.zeros((cols_out, rows_out, 6), jnp.float32)
                for piece_index in range(4):
                    step_col = piece_index // 2
                    step_row = piece_index % 2
                    hit = (shift_col + step_col == total_col) & (shift_row + step_row == total_row)
                    first_weight = level_index * 24 + piece_index * 6
                    piece_weights = weights[:, :, first_weight : first_weight + 6]
                    combined = combined + jnp.where(hit[:, :, None], piece_weights, 0.0)
                col_start = total_col + 2
                row_start = total_row + 2
                for moment_index in range(6):
                    window = moments[moment_index][
                        col_start : col_start + cols_out,
                        row_start : row_start + rows_out,
                        level_index,
                        :,
                    ]
                    summed = summed + combined[:, :, moment_index : moment_index + 1] * window
        results.append(summed)
    return jnp.stack(results, axis=2)


def orient_strip(strips, owner, codes, side_index, column_index):
    chosen = lax.dynamic_index_in_dim(strips, owner[side_index, column_index], 0, keepdims=False)
    code_value = codes[side_index, column_index]
    chosen = jnp.where(code_value % 2 == 1, chosen[::-1], chosen)
    return jnp.where(code_value // 2 % 2 == 1, chosen[:, ::-1], chosen)


def on_device(tracers, weights, offsets, owner, codes):
    rows_local = tracers.shape[1]
    extended = padded(tracers, (("gx", 0), ("gy", 1)), 3)
    column_index = lax.axis_index("gx")
    row_index = lax.axis_index("gy")
    last_row = lax.axis_size("gy") - 1
    lower_rows = extended[:, 3:6]
    upper_rows = extended[:, rows_local : rows_local + 3]
    lower_all, upper_all = sent_together((lower_rows[None], upper_rows[None]), "gx", 0, 1)
    below = orient_strip(lower_all, owner, codes, 0, column_index)
    above = orient_strip(upper_all, owner, codes, 1, column_index)
    bottom_rows = jnp.where(row_index == 0, below, extended[:, :3])
    top_rows = jnp.where(row_index == last_row, above, extended[:, rows_local + 3 :])
    extended = jnp.concatenate([bottom_rows, extended[:, 3 : rows_local + 3], top_rows], axis=1)
    return remap_block(extended, weights, offsets)


def solution(mesh):
    in_specs = (P("gx", "gy", None, None), P("gx", "gy", None), P("gx", "gy", None), P(), P())
    out_specs = P("gx", "gy", None, None)
    return jax.shard_map(
        on_device, mesh=mesh, in_specs=in_specs, out_specs=out_specs, check_vma=False
    )
```

profile of v0, /device:TPU:2, one launch (start us, length us, event | category | flops | bytes accessed | tf_op | source)
XLA Modules:
  0.0 508.7 jit_solution(11144718894114519758)
XLA Ops:
  6.6 1.3 copy.40
  7.9 0.8 fusion.682
  8.6 1.5 collective-permute-start
  10.1 0.8 collective-permute-start.1
  10.9 0.7 constant_dynamic-slice_fusion.1
  20.0 0.6 and_bitcast_fusion.97
  20.6 1.1 and_bitcast_fusion.96
  24.4 0.6 slice_bitcast_fusion.289
  25.0 0.6 slice_bitcast_fusion.295
  27.6 0.7 select_add_fusion.9
  29.6 0.7 copy-done.7
  30.5 0.6 fusion.681
  31.2 0.7 slice_bitcast_fusion.560
  31.9 0.7 pad_maximum_fusion.4
  32.7 1.4 slice_bitcast_fusion.313
  34.2 1.4 slice_bitcast_fusion.319
  35.6 0.8 select_add_fusion.12
  37.1 0.6 slice_bitcast_fusion.331
  38.4 0.8 select_add_fusion.15
  40.4 0.6 slice_bitcast_fusion.355
  41.0 0.8 select_add_fusion.18
  42.4 0.6 slice_bitcast_fusion.367
  43.1 0.6 slice_bitcast_fusion.373
  43.9 0.6 slice_bitcast_fusion.379
  44.5 0.6 slice_bitcast_fusion.385
  49.4 0.6 slice_bitcast_fusion.427
  50.1 0.6 slice_bitcast_fusion.433
  51.4 0.6 slice_bitcast_fusion.445
  52.0 0.6 slice_bitcast_fusion.451
  53.3 0.6 slice_bitcast_fusion.463
  56.6 0.6 slice_bitcast_fusion.493
  59.2 0.6 slice_bitcast_fusion.517
  62.5 0.6 slice_bitcast_fusion.547
  63.7 0.6 slice_bitcast_fusion.559
  64.4 5.8 %collective-permute-start.3 = (f32[18,3,2,128]{3,1,0,2:T(4,128)S(1)}, f32[18,3,2,128]{3,1,0,2:T(4,128)S(1)}, u32[]{:S(2)}, u32[]{:S(2)}) collective-permute-start(f32[18,3,2,128]{3,1,0,2:T(4,128)S(1)} %copy-done.12), channel_id=1, source_target_pairs={{1,0},{2,1},{3,2},{0,3},{5,4},{6,5},{7,6},{4,7},{9,8},{10,9},{11,1... | collective-permute-start | bytes 165896 | tf_op jit(solution)/shard_map/ppermute | solution.py:16
  70.2 1.1 constant_dynamic-update-slice_fusion.1
  71.3 1.0 copy-done.3
  72.3 0.7 constant_dynamic-update-slice_fusion.3
  73.0 323.1 %all-gather.2.cloned.1.call-done = f32[64,36,3,2,128]{4,3,2,1,0:T(2,128)} async-done(((f32[1,36,3,2,128]{4,3,2,1,0:T(2,128)}), f32[64,36,3,2,128]{4,3,2,1,0:T(2,128)}) %all-gather.2.cloned.1.call-update) | async-done | bytes 7077904 | tf_op jit(solution)/shard_map/all_gather | solution.py:29
  396.1 7.3 %fusion.680 = (f32[64,18,3,2,128]{4,3,2,1,0:T(2,128)}, f32[64,18,3,2,128]{4,3,2,1,0:T(2,128)S(1)}) fusion(f32[64,36,3,2,128]{4,3,2,1,0:T(2,128)} %all-gather.2.cloned.1.call-done), kind=kLoop, calls=%fused_computation.1584 | loop fusion | bytes 14155776 | tf_op jit(solution)/shard_map/split | solution.py:29
  403.7 4.0 fusion.14
  407.7 3.4 fusion.8
  411.1 3.3 fusion.2
  414.4 0.8 dynamic-slice_bitcast_fusion
  416.4 0.7 subtract_multiply_fusion.1
  417.8 39.6 %fusion.269 = f32[12,64,1,128]{3,1,0,2:T(8,128)S(1)} fusion(f32[16,68,2,128]{3,1,0,2:T(8,128)S(1)} %get-tuple-element.86, f32[16,68,2,128]{3,1,0,2:T(8,128)S(1)} %get-tuple-element.88, f32[16,68,2,128]{3,1,0,2:T(8,128)S(1)} %get-tuple-element.89, f32[16,68,2,128]{3,1,0,2:T(8,128)S(1)} %get-tuple-element.87, f32[16,68,2,128]{3,1,0,2:T(8,128)S(1)} %get-tuple-element.85, ...), kind=kLoop, calls=%fused_computation.337 | loop fusion | flops 30375936 | bytes 57139200 | tf_op jit(solution)/shard_map/stack | solution.py:79
  457.4 42.9 %fusion.456 = f32[12,64,1,128]{3,1,0,2:T(8,128)S(1)} fusion(f32[16,68,2,128]{3,1,0,2:T(8,128)S(1)} %get-tuple-element.86, f32[16,68,2,128]{3,1,0,2:T(8,128)S(1)} %get-tuple-element.88, f32[16,68,2,128]{3,1,0,2:T(8,128)S(1)} %get-tuple-element.89, f32[16,68,2,128]{3,1,0,2:T(8,128)S(1)} %get-tuple-element.87, f32[16,68,2,128]{3,1,0,2:T(8,128)S(1)} %get-tuple-element.85, ...), kind=kLoop, calls=%fused_computation.656 | loop fusion | flops 30375936 | bytes 57139200 | tf_op jit(solution)/shard_map/stack | solution.py:79
  500.4 1.5 copy.81
  (206 shorter events, 23.8 us)
Async XLA Ops:
  6.5 4.4 copy-start.64
  6.5 4.4 copy-start.65
  6.5 12.8 %copy-start.39 = (s32[12,64,4]{1,2,0:T(4,128)S(1)}, s32[12,64,4]{1,2,0:T(4,128)}, u32[]{:S(2)}) copy-start(s32[12,64,4]{1,2,0:T(4,128)} %param.7) | copy-start | bytes 36868
  6.5 12.8 %copy-start.11 = (f32[12,64,48]{1,2,0:T(8,128)S(1)}, f32[12,64,48]{1,2,0:T(8,128)}, u32[]{:S(2)}) copy-start(f32[12,64,48]{1,2,0:T(8,128)} %param.6) | copy-start | bytes 442372
  6.5 389.6 %all-gather.2.cloned.1.call-start = ((), (), s32[]{:S(2)}) async-start(), calls=%async_computation | async-start | bytes 7188480 | tf_op jit(solution)/shard_map/all_gather | solution.py:29
  7.9 13.8 %copy-start.1 = (f32[12,64,2,128]{3,1,0,2:T(8,128)}, f32[12,64,2,128]{3,1,0,2:T(8,128)S(1)}, u32[]{:S(2)}) copy-start(f32[12,64,2,128]{3,1,0,2:T(8,128)S(1)} %copy.40) | copy-start | bytes 2359300
  8.6 20.2 %collective-permute-start = (f32[3,64,2,128]{3,1,0,2:T(8,128)S(1)}, f32[3,64,2,128]{3,1,0,2:T(8,128)S(1)}, u32[]{:S(2)}, u32[]{:S(2)}) collective-permute-start(f32[3,64,2,128]{3,1,0,2:T(8,128)S(1)} %get-tuple-element.117), channel_id=1, source_target_pairs={{0,4},{4,8},{8,12},{12,16},{16,20},{20,24},{24,28},{28,32},{32,36}... | collective-permute-start | bytes 589832 | tf_op jit(solution)/shard_map/ppermute | solution.py:14
  10.1 19.0 %collective-permute-start.1 = (f32[3,64,2,128]{3,1,0,2:T(8,128)}, f32[3,64,2,128]{3,1,0,2:T(8,128)S(1)}, u32[]{:S(2)}, u32[]{:S(2)}) collective-permute-start(f32[3,64,2,128]{3,1,0,2:T(8,128)} %get-tuple-element.116), channel_id=1, source_target_pairs={{4,0},{8,4},{12,8},{16,12},{20,16},{24,20},{28,24},{32,28},{36,32}... | collective-permute-start | bytes 589832 | tf_op jit(solution)/shard_map/ppermute | solution.py:16
  21.7 7.3 %copy-start = (f32[12,64,2,128]{3,2,1,0:T(2,128)S(1)}, f32[12,64,2,128]{3,2,1,0:T(2,128)}, u32[]{:S(2)}) copy-start(f32[12,64,2,128]{3,2,1,0:T(2,128)} %param.5) | copy-start | bytes 2359300
  32.6 11.1 %copy-start.45 = (pred[12,64]{1,0:T(8,128)(4,1)S(1)}, pred[12,64]{1,0:T(8,128)(4,1)}, u32[]{:S(2)}) copy-start(pred[12,64]{1,0:T(8,128)(4,1)} %get-tuple-element.626) | copy-start | bytes 2308
  32.6 11.1 %copy-start.46 = (pred[12,64]{1,0:T(8,128)(4,1)S(1)}, pred[12,64]{1,0:T(8,128)(4,1)}, u32[]{:S(2)}) copy-start(pred[12,64]{1,0:T(8,128)(4,1)} %get-tuple-element.628) | copy-start | bytes 2308
  32.6 11.1 %copy-start.47 = (pred[12,64]{1,0:T(8,128)(4,1)S(1)}, pred[12,64]{1,0:T(8,128)(4,1)}, u32[]{:S(2)}) copy-start(pred[12,64]{1,0:T(8,128)(4,1)} %get-tuple-element.638) | copy-start | bytes 2308
  32.6 11.1 %copy-start.48 = (pred[12,64]{1,0:T(8,128)(4,1)S(1)}, pred[12,64]{1,0:T(8,128)(4,1)}, u32[]{:S(2)}) copy-start(pred[12,64]{1,0:T(8,128)(4,1)} %get-tuple-element.642) | copy-start | bytes 2308
  32.6 11.1 %copy-start.49 = (pred[12,64]{1,0:T(8,128)(4,1)S(1)}, pred[12,64]{1,0:T(8,128)(4,1)}, u32[]{:S(2)}) copy-start(pred[12,64]{1,0:T(8,128)(4,1)} %get-tuple-element.658) | copy-start | bytes 2308
  32.7 11.1 %copy-start.50 = (pred[12,64]{1,0:T(8,128)(4,1)S(1)}, pred[12,64]{1,0:T(8,128)(4,1)}, u32[]{:S(2)}) copy-start(pred[12,64]{1,0:T(8,128)(4,1)} %get-tuple-element.703) | copy-start | bytes 2308
  32.7 11.1 %copy-start.58 = (pred[12,64]{1,0:T(8,128)(4,1)S(1)}, pred[12,64]{1,0:T(8,128)(4,1)}, u32[]{:S(2)}) copy-start(pred[12,64]{1,0:T(8,128)(4,1)} %get-tuple-element.520) | copy-start | bytes 2308
  32.7 11.1 %copy-start.59 = (pred[12,64]{1,0:T(8,128)(4,1)S(1)}, pred[12,64]{1,0:T(8,128)(4,1)}, u32[]{:S(2)}) copy-start(pred[12,64]{1,0:T(8,128)(4,1)} %get-tuple-element.522) | copy-start | bytes 2308
  32.7 11.1 %copy-start.60 = (pred[12,64]{1,0:T(8,128)(4,1)S(1)}, pred[12,64]{1,0:T(8,128)(4,1)}, u32[]{:S(2)}) copy-start(pred[12,64]{1,0:T(8,128)(4,1)} %get-tuple-element.710) | copy-start | bytes 2308
  32.7 11.1 %copy-start.61 = (pred[12,64]{1,0:T(8,128)(4,1)S(1)}, pred[12,64]{1,0:T(8,128)(4,1)}, u32[]{:S(2)}) copy-start(pred[12,64]{1,0:T(8,128)(4,1)} %get-tuple-element.720) | copy-start | bytes 2308
  32.7 11.1 %copy-start.62 = (pred[12,64]{1,0:T(8,128)(4,1)S(1)}, pred[12,64]{1,0:T(8,128)(4,1)}, u32[]{:S(2)}) copy-start(pred[12,64]{1,0:T(8,128)(4,1)} %get-tuple-element.722) | copy-start | bytes 2308
  32.7 11.1 %copy-start.63 = (pred[12,64]{1,0:T(8,128)(4,1)S(1)}, pred[12,64]{1,0:T(8,128)(4,1)}, u32[]{:S(2)}) copy-start(pred[12,64]{1,0:T(8,128)(4,1)} %get-tuple-element.724) | copy-start | bytes 2308
  36.4 9.4 %copy-start.40 = (pred[12,64]{1,0:T(8,128)(4,1)S(1)}, pred[12,64]{1,0:T(8,128)(4,1)}, u32[]{:S(2)}) copy-start(pred[12,64]{1,0:T(8,128)(4,1)} %get-tuple-element.623) | copy-start | bytes 2308
  36.4 9.4 %copy-start.41 = (pred[12,64]{1,0:T(8,128)(4,1)S(1)}, pred[12,64]{1,0:T(8,128)(4,1)}, u32[]{:S(2)}) copy-start(pred[12,64]{1,0:T(8,128)(4,1)} %get-tuple-element.631) | copy-start | bytes 2308
  36.4 9.4 %copy-start.42 = (pred[12,64]{1,0:T(8,128)(4,1)S(1)}, pred[12,64]{1,0:T(8,128)(4,1)}, u32[]{:S(2)}) copy-start(pred[12,64]{1,0:T(8,128)(4,1)} %get-tuple-element.647) | copy-start | bytes 2308
  36.4 9.4 %copy-start.43 = (pred[12,64]{1,0:T(8,128)(4,1)S(1)}, pred[12,64]{1,0:T(8,128)(4,1)}, u32[]{:S(2)}) copy-start(pred[12,64]{1,0:T(8,128)(4,1)} %get-tuple-element.671) | copy-start | bytes 2308
  36.4 9.4 %copy-start.44 = (pred[12,64]{1,0:T(8,128)(4,1)S(1)}, pred[12,64]{1,0:T(8,128)(4,1)}, u32[]{:S(2)}) copy-start(pred[12,64]{1,0:T(8,128)(4,1)} %get-tuple-element.686) | copy-start | bytes 2308
  36.4 9.4 %copy-start.51 = (pred[12,64]{1,0:T(8,128)(4,1)S(1)}, pred[12,64]{1,0:T(8,128)(4,1)}, u32[]{:S(2)}) copy-start(pred[12,64]{1,0:T(8,128)(4,1)} %get-tuple-element.44) | copy-start | bytes 2308
  36.4 9.4 %copy-start.52 = (pred[12,64]{1,0:T(8,128)(4,1)S(1)}, pred[12,64]{1,0:T(8,128)(4,1)}, u32[]{:S(2)}) copy-start(pred[12,64]{1,0:T(8,128)(4,1)} %get-tuple-element.49) | copy-start | bytes 2308
  36.4 9.4 %copy-start.53 = (pred[12,64]{1,0:T(8,128)(4,1)S(1)}, pred[12,64]{1,0:T(8,128)(4,1)}, u32[]{:S(2)}) copy-start(pred[12,64]{1,0:T(8,128)(4,1)} %get-tuple-element.712) | copy-start | bytes 2308
  36.4 9.4 %copy-start.54 = (pred[12,64]{1,0:T(8,128)(4,1)S(1)}, pred[12,64]{1,0:T(8,128)(4,1)}, u32[]{:S(2)}) copy-start(pred[12,64]{1,0:T(8,128)(4,1)} %get-tuple-element.714) | copy-start | bytes 2308
  36.4 9.4 %copy-start.55 = (pred[12,64]{1,0:T(8,128)(4,1)S(1)}, pred[12,64]{1,0:T(8,128)(4,1)}, u32[]{:S(2)}) copy-start(pred[12,64]{1,0:T(8,128)(4,1)} %get-tuple-element.716) | copy-start | bytes 2308
  36.5 9.4 %copy-start.56 = (pred[12,64]{1,0:T(8,128)(4,1)S(1)}, pred[12,64]{1,0:T(8,128)(4,1)}, u32[]{:S(2)}) copy-start(pred[12,64]{1,0:T(8,128)(4,1)} %get-tuple-element.718) | copy-start | bytes 2308
  36.5 9.4 %copy-start.57 = (pred[12,64]{1,0:T(8,128)(4,1)S(1)}, pred[12,64]{1,0:T(8,128)(4,1)}, u32[]{:S(2)}) copy-start(pred[12,64]{1,0:T(8,128)(4,1)} %get-tuple-element.726) | copy-start | bytes 2308
  56.6 7.8 %copy-start.12 = (f32[18,3,2,128]{3,1,0,2:T(4,128)S(1)}, f32[18,3,2,128]{3,1,0,2:T(4,128)}, u32[]{:S(2)}) copy-start(f32[18,3,2,128]{3,1,0,2:T(4,128)} %get-tuple-element.113) | copy-start | bytes 165892
  56.6 13.6 %copy-start.13 = (f32[18,3,2,128]{3,2,1,0:T(2,128)S(1)}, f32[18,3,2,128]{3,2,1,0:T(2,128)}, u32[]{:S(2)}) copy-start(f32[18,3,2,128]{3,2,1,0:T(2,128)} %get-tuple-element.110) | copy-start | bytes 165892
  56.6 13.6 %copy-start.10 = (f32[3,64,2,128]{3,1,0,2:T(8,128)S(1)}, f32[3,64,2,128]{3,1,0,2:T(8,128)}, u32[]{:S(2)}) copy-start(f32[3,64,2,128]{3,1,0,2:T(8,128)} %copy-done.9) | copy-start | bytes 589828
  64.4 339.3 %collective-permute-start.3 = (f32[18,3,2,128]{3,1,0,2:T(4,128)S(1)}, f32[18,3,2,128]{3,1,0,2:T(4,128)S(1)}, u32[]{:S(2)}, u32[]{:S(2)}) collective-permute-start(f32[18,3,2,128]{3,1,0,2:T(4,128)S(1)} %copy-done.12), channel_id=1, source_target_pairs={{1,0},{2,1},{3,2},{0,3},{5,4},{6,5},{7,6},{4,7},{9,8},{10,9},{11,1... | collective-permute-start | bytes 165896 | tf_op jit(solution)/shard_map/ppermute | solution.py:16
  70.2 345.7 %collective-permute-start.2 = (f32[18,3,2,128]{3,2,1,0:T(2,128)S(1)}, f32[18,3,2,128]{3,2,1,0:T(2,128)}, u32[]{:S(2)}, u32[]{:S(2)}) collective-permute-start(f32[18,3,2,128]{3,2,1,0:T(2,128)S(1)} %copy-done.13), channel_id=1, source_target_pairs={{0,1},{1,2},{2,3},{3,0},{4,5},{5,6},{6,7},{7,4},{8,9},{9,10},{10,1... | collective-permute-start | bytes 165896 | tf_op jit(solution)/shard_map/ppermute | solution.py:14
  70.2 2.1 copy-start.8
  416.2 1.4 copy-start.4
  416.2 1.4 copy-start.14
  416.2 1.4 copy-start.15
  416.2 1.4 copy-start.16
  416.2 1.4 copy-start.17
  416.2 1.4 copy-start.18
  416.2 1.4 copy-start.19
  417.8 39.6 %copy-start.5 = (f32[12,64,1,128]{3,2,1,0:T(1,128)S(1)}, f32[12,64,1,128]{3,2,1,0:T(1,128)}, u32[]{:S(2)}) copy-start(f32[12,64,1,128]{3,2,1,0:T(1,128)} %get-tuple-element.97) | copy-start | bytes 1179652
  417.8 39.6 %copy-start.6 = (f32[12,64,1,128]{3,2,1,0:T(1,128)S(1)}, f32[12,64,1,128]{3,2,1,0:T(1,128)}, u32[]{:S(2)}) copy-start(f32[12,64,1,128]{3,2,1,0:T(1,128)} %get-tuple-element.98) | copy-start | bytes 1179652
  (23 other events, 30.0 us)
Sparse Core Ops, SparseCore 0:
  32.7 363.3 all-gather.1
where the time goes:
time: 509 us
  waiting for transfers between devices  323 us (63%)
  other arithmetic  102 us (20%)
  local copies, waits for them, and re-layouts  52.1 us (10%)
  between operations  23.6 us (5%)
  starting transfers between devices  8.13 us (2%)
    all_gather x1, waiting for transfers between devices, sent_together(): lax.all_gather(both, axis, axis=dim, tiled=True)  323 us
    another operation x3, other arithmetic, remap_block(): return jnp.stack(results, axis=2)  82.5 us
    mul x50, local copies, waits for them, and re-layouts, remap_block(): summed = summed + combined[:, :, moment_index:moment_index + 1] * window  33.1 us
    concatenate x5, other arithmetic, on_device(): jnp.concatenate([bottom_rows, extended[:, 3:rows_local + 3], top_rows], a...  11.5 us
  transfers between devices with their start and end apart: 5, of which 1 were waited for; matrix products, arithmetic and copies ran while one was open for 12% of the time, Pallas kernels for 0%

commit v1 on v0

v1 whole, which is shorter than its diff:
```python
import functools

import jax
import jax.numpy as jnp
from jax import lax
from jax.experimental import pallas as pl
from jax.experimental.pallas import tpu as pltpu
from jax.sharding import PartitionSpec as P

MESH = pl.DeviceIdType.MESH
F32, BF16 = jnp.float32, jnp.bfloat16
COLS, ROWS, HALO = 12, 64, 3
EXT = COLS + 2 * HALO
PAIRS = 2 * HALO
LINES = 2 * ROWS
TOP = LINES + PAIRS
TALL = 144
BANDS = 8
GROUPS = ((3, 6), (0, 3), (9, 3))


def stencil_rows():
    rows = []
    for i in range(4):
        for j in range(8):
            rows.append([0.0] * 24)
    for a in range(2):
        for e in range(2):
            for k, taps in enumerate((
                {(0, 0): 1.0},
                {(1, 0): 0.5, (-1, 0): -0.5},
                {(0, 1): 0.5, (0, -1): -0.5},
                {(1, 0): 0.5, (0, 0): -1.0, (-1, 0): 0.5},
                {(0, 1): 0.5, (0, 0): -1.0, (0, -1): 0.5},
                {(1, 1): 0.25, (1, -1): -0.25, (-1, 1): -0.25, (-1, -1): 0.25},
            )):
                for (u, v), value in taps.items():
                    rows[(a + 1 + u) * 8 + e + 1 + v][6 * (2 * a + e) + k] += value
    return rows


def halves(value):
    high = value.astype(BF16)
    return high, (value - high.astype(F32)).astype(BF16)


def matrices(weights, offsets, taps, flat, tall, mats):
    for x in range(COLS):
        w = weights[x]
        flat[:, 128 * x : 128 * x + 128] = jnp.concatenate([w[:24], w[24:]], axis=1)
    tall[...] = jnp.zeros_like(tall)
    coefs = jnp.dot(taps[...], flat[...], precision=lax.Precision.HIGHEST, preferred_element_type=F32)
    row = lax.broadcasted_iota(jnp.int32, (8, 128), 0)
    inner = lax.broadcasted_iota(jnp.int32, (8, 128), 1) % 8
    for first, count in GROUPS:
        for xl in range(count):
            x = first + xl
            o = offsets[x]
            cols = jnp.concatenate([o[0:1], o[2:3]], axis=1) + 2
            lines = jnp.concatenate([o[1:2], o[3:4]], axis=1) + 2
            shift = jnp.broadcast_to(lines, (8, 128)) + inner
            steps = jnp.broadcast_to(cols, (8, 128))
            pick = (row - shift) & 7
            in_low = row >= shift
            in_high = (row < shift) & (shift <= row + 8)
            zero = jnp.zeros((8, 128), F32)
            low, high = [], []
            for i in range(4):
                turned = jnp.take_along_axis(coefs[8 * i : 8 * i + 8, 128 * x : 128 * x + 128], pick, axis=0)
                low.append(jnp.where(in_low, turned, zero))
                high.append(jnp.where(in_high, turned, zero))
            odd, two = (steps & 1) == 1, steps >= 2
            for part, pieces in enumerate((low, high)):
                pieces = [zero] + pieces + [zero]
                once = [jnp.where(odd, pieces[d], pieces[d + 1]) for d in range(5)]
                once = [zero, zero] + once + [zero, zero]
                for d in range(7):
                    at = 16 * (xl + d) + 8 * part
                    tall[x, at : at + 8, :] = jnp.where(two, once[d], once[d + 2])
    for x in range(COLS):
        mats[:, :, 8 * x : 8 * x + 8, :] = jnp.transpose(tall[x]).reshape(2, BANDS, 8, 256)


def remap(bands, groups, field, mats, out):
    def band(step, carry):
        b = bands[0] + step * (bands[1] - bands[0] if len(bands) > 1 else 1)
        base = pl.multiple_of(16 * b, 16)
        for first, count in groups:
            depth = 16 * (count + PAIRS)
            for level in range(2):
                mat = mats[level, b, 8 * first : 8 * (first + count), :depth]
                mat_high, mat_low = halves(mat)
                cells = field[first : first + count + PAIRS, pl.ds(base + level, 16, 2), :]
                cell_high, cell_low = halves(cells.reshape(depth, 128))
                both = jnp.dot(mat_high, jnp.concatenate([cell_high, cell_low], axis=1), preferred_element_type=F32)
                result = both[:, :128] + both[:, 128:] + jnp.dot(mat_low, cell_high, preferred_element_type=F32)
                for xl in range(count):
                    out[first + xl, pl.ds(base + level, 8, 2), :] = result[8 * xl : 8 * xl + 8]
        return carry

    lax.fori_loop(0, len(bands), band, 0, unroll=True)


def kernel(
    owner, codes, tracers, weights_in, offsets_in, taps, out,
    field, weights, offsets, flat, tall, mats, gathered, chosen, landed,
    in_sem, side_send, side_recv, row_send, row_recv, all_send, all_recv, last_send, last_recv,
):
    gx, gy = lax.axis_index("gx"), lax.axis_index("gy")
    y, z, x = gx // 16, (gx // 4) % 4, gx % 4
    east, west = (gx + 1) % 64, (gx + 63) % 64
    edge = (gy == 0) | (gy == 3)
    me = y * 4 + x

    def peer(step):
        p = (me + step) % 16
        return (p // 4) * 16 + z * 4 + p % 4

    def along(step):
        return y * 16 + ((z + step) % 4) * 4 + x

    loads = [
        pltpu.make_async_copy(weights_in, weights, in_sem.at[0]),
        pltpu.make_async_copy(offsets_in, offsets, in_sem.at[1]),
        pltpu.make_async_copy(tracers, field.at[HALO : HALO + COLS, PAIRS:TOP, :], in_sem.at[2]),
    ]
    for load in loads:
        load.start()

    barrier = pltpu.get_barrier_semaphore()

    def greet(to_x, to_y):
        pl.semaphore_signal(barrier, inc=1, device_id=(to_x, to_y), device_id_type=MESH)

    greet(east, gy)
    greet(west, gy)

    @pl.when(gy > 0)
    def _():
        for to in (west, gx, east):
            greet(to, gy - 1)

    @pl.when(gy < 3)
    def _():
        for to in (west, gx, east):
            greet(to, gy + 1)

    @pl.when(edge)
    def _():
        for step in range(1, 16):
            greet(peer(step), gy)
        for step in range(1, 4):
            greet(along(step), gy)
        pl.semaphore_wait(barrier, 23)

    @pl.when(jnp.logical_not(edge))
    def _():
        pl.semaphore_wait(barrier, 8)

    def send(source, target, send_sem, recv_sem, to):
        return pltpu.make_async_remote_copy(
            src_ref=source, dst_ref=target, send_sem=send_sem, recv_sem=recv_sem, device_id=to, device_id_type=MESH
        )

    edge_at = jnp.where(gy == 0, 0, LINES - PAIRS)
    strip = tracers.at[:, pl.ds(edge_at, PAIRS), :]

    def gather_copy(step):
        return send(
            strip, gathered.at[me, :, 0:PAIRS, :], all_send.at[step], all_recv.at[me], (peer(step), gy)
        )

    def gather_wait(step):
        p = (me + step) % 16
        return send(
            strip, gathered.at[p, :, 0:PAIRS, :], all_send.at[step], all_recv.at[p], (peer(step), gy)
        )

    own_strip = pltpu.make_async_copy(strip, gathered.at[me, :, 0:PAIRS, :], in_sem.at[3])

    @pl.when(edge)
    def _():
        own_strip.start()
        for step in range(1, 16):
            gather_copy(step).start()

    def row_copies(up):
        source = pl.ds(LINES - PAIRS, PAIRS) if up else pl.ds(0, PAIRS)
        target = pl.ds(0, PAIRS) if up else pl.ds(TOP, PAIRS)
        to = gy + 1 if up else gy - 1
        base = 0 if up else 3
        return [
            send(tracers.at[:, source, :], field.at[HALO : HALO + COLS, target, :],
                 row_send.at[base], row_recv.at[base], (gx, to)),
            send(tracers.at[0:HALO, source, :], field.at[HALO + COLS : EXT, target, :],
                 row_send.at[base + 1], row_recv.at[base + 1], (west, to)),
            send(tracers.at[COLS - HALO : COLS, source, :], field.at[0:HALO, target, :],
                 row_send.at[base + 2], row_recv.at[base + 2], (east, to)),
        ]

    @pl.when(gy < 3)
    def _():
        for copy in row_copies(True):
            copy.start()

    @pl.when(gy > 0)
    def _():
        for copy in row_copies(False):
            copy.start()

    to_west = send(tracers.at[0:HALO], field.at[HALO + COLS : EXT, PAIRS:TOP, :], side_send.at[0], side_recv.at[0], (west, gy))
    to_east = send(tracers.at[COLS - HALO : COLS], field.at[0:HALO, PAIRS:TOP, :], side_send.at[1], side_recv.at[1], (east, gy))
    to_west.start()
    to_east.start()

    for c in range(EXT):
        field[c, TOP + PAIRS : TALL, :] = jnp.zeros((TALL - TOP - PAIRS, 128), F32)

    loads[0].wait()
    loads[1].wait()
    matrices(weights, offsets, taps, flat, tall, mats)
    loads[2].wait()

    side = jnp.where(gy == 0, 0, 1)

    def index_of(block):
        return (block // 16) * 4 + block % 4

    def last_copy(step):
        return send(
            chosen.at[step, :, 0:PAIRS, :], landed.at[z, :, 0:PAIRS, :],
            last_send.at[step], last_recv.at[z], (along(step), gy),
        )

    def last_wait(step):
        p = (z + step) % 4
        return send(
            chosen.at[step, :, 0:PAIRS, :], landed.at[p, :, 0:PAIRS, :],
            last_send.at[step], last_recv.at[p], (along(step), gy),
        )

    @pl.when(edge)
    def _():
        own_strip.wait()
        for step in range(1, 16):
            gather_wait(step).wait_recv()
        for step in (1, 2, 3, 0):
            block = owner[side, along(step)]
            mid = gathered[index_of(block), :, 0:PAIRS, :]
            left = gathered[index_of((block + 63) % 64), COLS - HALO : COLS, 0:PAIRS, :]
            right = gathered[index_of((block + 1) % 64), 0:HALO, 0:PAIRS, :]
            if step:
                chosen[step, 0:HALO, 0:PAIRS, :] = left
                chosen[step, HALO : HALO + COLS, 0:PAIRS, :] = mid
                chosen[step, HALO + COLS : EXT, 0:PAIRS, :] = right
                last_copy(step).start()
            else:
                landed[z, 0:HALO, 0:PAIRS, :] = left
                landed[z, HALO : HALO + COLS, 0:PAIRS, :] = mid
                landed[z, HALO + COLS : EXT, 0:PAIRS, :] = right

    remap((1, 2, 3, 4, 5, 6), GROUPS[:1], field, mats, out)
    to_west.wait()
    to_east.wait()
    remap((1, 2, 3, 4, 5, 6), GROUPS[1:], field, mats, out)

    @pl.when(gy > 0)
    def _():
        for copy in row_copies(True):
            copy.wait_recv()

    @pl.when(gy < 3)
    def _():
        for copy in row_copies(False):
            copy.wait_recv()

    @pl.when(edge)
    def _():
        for step in range(1, 4):
            last_wait(step).wait_recv()
        block = owner[side, gx]
        code = codes[side, gx]
        turn, flip = code % 2, (code // 2) % 2

        def level_of(b):
            return (b // 4) % 4

        zs = (level_of((block + 63) % 64), level_of(block), level_of((block + 1) % 64))
        for u in range(EXT):
            v = jnp.where(turn == 1, EXT - 1 - u, u)
            west_z, east_z = (zs[0], zs[2])
            if u < HALO:
                part = jnp.where(turn == 1, east_z, west_z)
            elif u < HALO + COLS:
                part = zs[1]
            else:
                part = jnp.where(turn == 1, west_z, east_z)
            piece = landed[part, v, 0:PAIRS, :]
            back = jnp.concatenate([piece[4:6], piece[2:4], piece[0:2]], axis=0)
            piece = jnp.where(flip == 1, back, piece)

            @pl.when(gy == 0)
            def _():
                field[u, 0:PAIRS, :] = piece

            @pl.when(gy == 3)
            def _():
                field[u, TOP : TOP + PAIRS, :] = piece

    remap((0, 7), GROUPS, field, mats, out)

    @pl.when(gy < 3)
    def _():
        for copy in row_copies(True):
            copy.wait_send()

    @pl.when(gy > 0)
    def _():
        for copy in row_copies(False):
            copy.wait_send()

    @pl.when(edge)
    def _():
        for step in range(1, 16):
            gather_copy(step).wait_send()
        for step in range(1, 4):
            last_copy(step).wait_send()


def on_device(tracers, weights, offsets, owner, codes):
    lines = tracers.reshape(COLS, LINES, 128)
    taps = jnp.array(stencil_rows(), F32)
    any_space = pl.BlockSpec(memory_space=pl.ANY)
    smem = pl.BlockSpec(memory_space=pltpu.SMEM)
    vmem = pl.BlockSpec(memory_space=pltpu.VMEM)
    dma = pltpu.SemaphoreType.DMA
    result = pl.pallas_call(
        kernel,
        out_shape=jax.ShapeDtypeStruct((COLS, LINES, 128), F32),
        in_specs=[smem, smem, any_space, any_space, any_space, vmem],
        out_specs=vmem,
        scratch_shapes=[
            pltpu.VMEM((EXT, TALL, 128), F32),
            pltpu.VMEM((COLS, 48, ROWS), F32),
            pltpu.VMEM((COLS, 4, ROWS), jnp.int32),
            pltpu.VMEM((24, 128 * COLS), F32),
            pltpu.VMEM((COLS, 256, 128), F32),
            pltpu.VMEM((2, BANDS, 8 * COLS, 256), F32),
            pltpu.VMEM((16, COLS, 8, 128), F32),
            pltpu.VMEM((4, EXT, 8, 128), F32),
            pltpu.VMEM((4, EXT, 8, 128), F32),
            dma((4,)), dma((2,)), dma((2,)), dma((6,)), dma((6,)), dma((16,)), dma((16,)), dma((4,)), dma((4,)),
        ],
        compiler_params=pltpu.CompilerParams(
            collective_id=0, has_side_effects=True, vmem_limit_bytes=40 * 1024 * 1024
        ),
    )(owner, codes, lines, jnp.transpose(weights, (0, 2, 1)), jnp.transpose(offsets, (0, 2, 1)), taps)
    return result.reshape(COLS, ROWS, 2, 128)


def solution(mesh):
    in_specs = (P("gx", "gy", None, None), P("gx", "gy", None), P("gx", "gy", None), P(), P())
    return jax.shard_map(
        on_device, mesh=mesh, in_specs=in_specs, out_specs=P("gx", "gy", None, None), check_vma=False
    )
```

time: 509 us -> 29.9 us (0.06)
  the two profiles are of different devices: /device:TPU:2 before, /device:TPU:6 now
where the time goes in v1:
time: 29.9 us; the launch traced here: 29.6 us
  Pallas kernels  24.4 us (82%)
  local copies, waits for them, and re-layouts  5.12 us (17%)
    pallas_call x1, Pallas kernels, on_device(): pl.pallas_call(kernel, out_shape=jax.ShapeDtypeStruct((COLS, LINES, 128),...  24.4 us
    unnamed x13, local copies, waits for them, and re-layouts  5.12 us

profile of v1, /device:TPU:6, one launch (start us, length us, event | category | flops | bytes accessed | tf_op | source)
XLA Modules:
  0.0 29.6 jit_solution(11486636795104127732)
XLA Ops:
  0.0 0.0 copy-start.5
  0.0 0.0 copy-start.4
  0.0 0.7 %copy-done.5 = s32[2,64]{1,0:T(2,128)S(1)} copy-done((s32[2,64]{1,0:T(2,128)S(1)}, s32[2,64]{1,0:T(2,128)}, u32[]{:S(2)}) %copy-start.5) | copy-done | bytes 536
  0.7 0.0 copy-done.4
  0.7 0.0 copy-start
  0.7 1.1 %copy-done = f32[12,64,2,128]{3,2,1,0:T(2,128)S(1)} copy-done((f32[12,64,2,128]{3,2,1,0:T(2,128)S(1)}, f32[12,64,2,128]{3,2,1,0:T(2,128)}, u32[]{:S(2)}) %copy-start) | copy-done | bytes 786456
  1.8 0.0 copy-start.1
  1.8 1.0 %copy-done.1 = f32[12,64,48]{1,2,0:T(8,128)S(1)} copy-done((f32[12,64,48]{1,2,0:T(8,128)S(1)}, f32[12,64,48]{1,2,0:T(8,128)}, u32[]{:S(2)}) %copy-start.1) | copy-done | bytes 147480
  2.8 0.0 copy-start.2
  2.8 0.7 %copy-done.2 = s32[12,64,4]{1,2,0:T(4,128)S(1)} copy-done((s32[12,64,4]{1,2,0:T(4,128)S(1)}, s32[12,64,4]{1,2,0:T(4,128)}, u32[]{:S(2)}) %copy-start.2) | copy-done | bytes 12312
  3.5 0.0 copy-start.3
  3.5 0.7 %copy-done.3 = f32[32,24]{1,0:T(8,128)S(1)} copy-done((f32[32,24]{1,0:T(8,128)S(1)}, f32[32,24]{1,0:T(8,128)}, u32[]{:S(2)}) %copy-start.3) | copy-done | bytes 3096
  4.2 24.4 %shard_map.64 = f32[12,128,128]{2,1,0:T(8,128)S(1)} custom-call(s32[2,64]{1,0:T(2,128)S(1)} %copy-done.4, s32[2,64]{1,0:T(2,128)S(1)} %copy-done.5, f32[12,128,128]{2,1,0:T(8,128)S(1)} %bitcast.5, f32[12,48,64]{2,1,0:T(8,128)S(1)} %bitcast.6, s32[12,4,64]{2,1,0:T(4,128)S(1)} %bitcast.7, f32[32,24]{1,0:T(8,128)S(1)} %copy-done.3), custom_call_target="tpu_custom_call" | custom-call | tf_op jit(solution)/shard_map/pallas_call | solution.py:337
  28.7 0.9 %copy.8 = f32[12,64,2,128]{3,2,1,0:T(2,128)} copy(f32[12,64,2,128]{3,2,1,0:T(2,128)S(1)} %bitcast.4) | data formatting | bytes 1572864
Async XLA Ops:
  0.0 0.7 %copy-start.5 = (s32[2,64]{1,0:T(2,128)S(1)}, s32[2,64]{1,0:T(2,128)}, u32[]{:S(2)}) copy-start(s32[2,64]{1,0:T(2,128)} %codes.1) | copy-start | bytes 1540
  0.0 0.7 %copy-start.4 = (s32[2,64]{1,0:T(2,128)S(1)}, s32[2,64]{1,0:T(2,128)}, u32[]{:S(2)}) copy-start(s32[2,64]{1,0:T(2,128)} %owner.1) | copy-start | bytes 1540
  0.7 1.1 %copy-start = (f32[12,64,2,128]{3,2,1,0:T(2,128)S(1)}, f32[12,64,2,128]{3,2,1,0:T(2,128)}, u32[]{:S(2)}) copy-start(f32[12,64,2,128]{3,2,1,0:T(2,128)} %param.6) | copy-start | bytes 2359300
  1.8 1.0 %copy-start.1 = (f32[12,64,48]{1,2,0:T(8,128)S(1)}, f32[12,64,48]{1,2,0:T(8,128)}, u32[]{:S(2)}) copy-start(f32[12,64,48]{1,2,0:T(8,128)} %param.7) | copy-start | bytes 442372
  2.8 0.7 %copy-start.2 = (s32[12,64,4]{1,2,0:T(4,128)S(1)}, s32[12,64,4]{1,2,0:T(4,128)}, u32[]{:S(2)}) copy-start(s32[12,64,4]{1,2,0:T(4,128)} %param.8) | copy-start | bytes 36868
  3.5 0.7 %copy-start.3 = (f32[32,24]{1,0:T(8,128)S(1)}, f32[32,24]{1,0:T(8,128)}, u32[]{:S(2)}) copy-start(f32[32,24]{1,0:T(8,128)} %constant.2.clone.taps) | copy-start | bytes 9220

commit v2 on v1

--- a/solution.py
+++ b/solution.py
@@ -19,24 +19,22 @@
 GROUPS = ((3, 6), (0, 3), (9, 3))
 
 
-def stencil_rows():
-    rows = []
-    for i in range(4):
-        for j in range(8):
-            rows.append([0.0] * 24)
-    for a in range(2):
-        for e in range(2):
-            for k, taps in enumerate((
-                {(0, 0): 1.0},
-                {(1, 0): 0.5, (-1, 0): -0.5},
-                {(0, 1): 0.5, (0, -1): -0.5},
-                {(1, 0): 0.5, (0, 0): -1.0, (-1, 0): 0.5},
-                {(0, 1): 0.5, (0, 0): -1.0, (0, -1): 0.5},
-                {(1, 1): 0.25, (1, -1): -0.25, (-1, 1): -0.25, (-1, -1): 0.25},
-            )):
-                for (u, v), value in taps.items():
-                    rows[(a + 1 + u) * 8 + e + 1 + v][6 * (2 * a + e) + k] += value
-    return rows
+def stencil():
+    shape = (32, 24)
+    tap, term = (lax.broadcasted_iota(jnp.int32, shape, dim) for dim in range(2))
+    piece, kind = term // 6, term % 6
+    u, v = tap // 8 - piece // 2 - 1, tap % 8 - piece % 2 - 1
+    near_u, near_v = jnp.abs(u) <= 1, jnp.abs(v) <= 1
+    on_u, on_v = near_u & (v == 0), near_v & (u == 0)
+    uf, vf = u.astype(F32), v.astype(F32)
+    zero = jnp.zeros(shape, F32)
+    centre = jnp.where((u == 0) & (v == 0), 1.0, zero)
+    value = jnp.where(kind == 0, centre, zero)
+    value = jnp.where((kind == 1) & on_u, 0.5 * uf, value)
+    value = jnp.where((kind == 2) & on_v, 0.5 * vf, value)
+    value = jnp.where((kind == 3) & on_u, 0.5 - 1.5 * centre, value)
+    value = jnp.where((kind == 4) & on_v, 0.5 - 1.5 * centre, value)
+    return jnp.where((kind == 5) & near_u & near_v, 0.25 * uf * vf, value)
 
 
 def halves(value):
@@ -44,12 +42,12 @@
     return high, (value - high.astype(F32)).astype(BF16)
 
 
-def matrices(weights, offsets, taps, flat, tall, mats):
+def matrices(weights, offsets, flat, tall, mats):
     for x in range(COLS):
         w = weights[x]
         flat[:, 128 * x : 128 * x + 128] = jnp.concatenate([w[:24], w[24:]], axis=1)
     tall[...] = jnp.zeros_like(tall)
-    coefs = jnp.dot(taps[...], flat[...], precision=lax.Precision.HIGHEST, preferred_element_type=F32)
+    coefs = jnp.dot(stencil(), flat[...], precision=lax.Precision.HIGHEST, preferred_element_type=F32)
     row = lax.broadcasted_iota(jnp.int32, (8, 128), 0)
     inner = lax.broadcasted_iota(jnp.int32, (8, 128), 1) % 8
     for first, count in GROUPS:
@@ -102,8 +100,8 @@
 
 
 def kernel(
-    owner, codes, tracers, weights_in, offsets_in, taps, out,
-    field, weights, offsets, flat, tall, mats, gathered, chosen, landed,
+    owner_in, codes_in, tracers, weights_in, offsets_in, out,
+    owner, codes, field, weights, offsets, flat, tall, mats, gathered, chosen, landed,
     in_sem, side_send, side_recv, row_send, row_recv, all_send, all_recv, last_send, last_recv,
 ):
     gx, gy = lax.axis_index("gx"), lax.axis_index("gy")
@@ -122,6 +120,8 @@
     loads = [
         pltpu.make_async_copy(weights_in, weights, in_sem.at[0]),
         pltpu.make_async_copy(offsets_in, offsets, in_sem.at[1]),
+        pltpu.make_async_copy(owner_in, owner, in_sem.at[4]),
+        pltpu.make_async_copy(codes_in, codes, in_sem.at[5]),
         pltpu.make_async_copy(tracers, field.at[HALO : HALO + COLS, PAIRS:TOP, :], in_sem.at[2]),
     ]
     for load in loads:
@@ -218,8 +218,9 @@
 
     loads[0].wait()
     loads[1].wait()
-    matrices(weights, offsets, taps, flat, tall, mats)
-    loads[2].wait()
+    matrices(weights, offsets, flat, tall, mats)
+    for load in loads[2:]:
+        load.wait()
 
     side = jnp.where(gy == 0, 0, 1)
 
@@ -329,17 +330,17 @@
 
 def on_device(tracers, weights, offsets, owner, codes):
     lines = tracers.reshape(COLS, LINES, 128)
-    taps = jnp.array(stencil_rows(), F32)
-    any_space = pl.BlockSpec(memory_space=pl.ANY)
-    smem = pl.BlockSpec(memory_space=pltpu.SMEM)
+    hbm = pl.BlockSpec(memory_space=pltpu.HBM)
     vmem = pl.BlockSpec(memory_space=pltpu.VMEM)
     dma = pltpu.SemaphoreType.DMA
     result = pl.pallas_call(
         kernel,
         out_shape=jax.ShapeDtypeStruct((COLS, LINES, 128), F32),
-        in_specs=[smem, smem, any_space, any_space, any_space, vmem],
+        in_specs=[hbm] * 5,
         out_specs=vmem,
         scratch_shapes=[
+            pltpu.SMEM((2, 64), jnp.int32),
+            pltpu.SMEM((2, 64), jnp.int32),
             pltpu.VMEM((EXT, TALL, 128), F32),
             pltpu.VMEM((COLS, 48, ROWS), F32),
             pltpu.VMEM((COLS, 4, ROWS), jnp.int32),
@@ -349,12 +350,12 @@
             pltpu.VMEM((16, COLS, 8, 128), F32),
             pltpu.VMEM((4, EXT, 8, 128), F32),
             pltpu.VMEM((4, EXT, 8, 128), F32),
-            dma((4,)), dma((2,)), dma((2,)), dma((6,)), dma((6,)), dma((16,)), dma((16,)), dma((4,)), dma((4,)),
+            dma((6,)), dma((2,)), dma((2,)), dma((6,)), dma((6,)), dma((16,)), dma((16,)), dma((4,)), dma((4,)),
         ],
         compiler_params=pltpu.CompilerParams(
             collective_id=0, has_side_effects=True, vmem_limit_bytes=40 * 1024 * 1024
         ),
-    )(owner, codes, lines, jnp.transpose(weights, (0, 2, 1)), jnp.transpose(offsets, (0, 2, 1)), taps)
+    )(*(pltpu.with_memory_space_constraint(a, pltpu.HBM) for a in (owner, codes, lines, jnp.transpose(weights, (0, 2, 1)), jnp.transpose(offsets, (0, 2, 1)))))
     return result.reshape(COLS, ROWS, 2, 128)
 
 

time: 29.9 us -> 25 us (0.84)
  local copies, waits for them, and re-layouts: 5.12 us -> 0.88 us
  Pallas kernels: 24.4 us -> 24 us
    unnamed x13 -> x1, local copies, waits for them, and re-layouts: 5.12 us -> 0.88 us
    pallas_call x1, Pallas kernels: 24.4 us -> 24 us  [on_device(): pl.pallas_call(kernel, out_shape=jax.ShapeDtypeStruct((COLS, LINES, 128),...]
where the time goes in v2:
time: 25 us; the launch traced here: 24.9 us
  Pallas kernels  24 us (96%)
  local copies, waits for them, and re-layouts  0.88 us (4%)
    pallas_call x1, Pallas kernels, on_device(): pl.pallas_call(kernel, out_shape=jax.ShapeDtypeStruct((COLS, LINES, 128),...  24 us
    unnamed x1, local copies, waits for them, and re-layouts  0.88 us

profile of v2, /device:TPU:6, one launch (start us, length us, event | category | flops | bytes accessed | tf_op | source)
XLA Modules:
  0.0 24.9 jit_solution(11536889643819389842)
XLA Ops:
  0.0 24.0 %shard_map.55 = f32[12,128,128]{2,1,0:T(8,128)S(1)} custom-call(s32[2,64]{1,0:T(2,128)} %owner_in.1, s32[2,64]{1,0:T(2,128)} %codes_in.1, f32[12,128,128]{2,1,0:T(8,128)} %bitcast.5, f32[12,48,64]{2,1,0:T(8,128)} %bitcast.6, s32[12,4,64]{2,1,0:T(4,128)} %bitcast.7), custom_call_target="tpu_custom_call" | custom-call | tf_op jit(solution)/shard_map/pallas_call | solution.py:336
  24.0 0.9 %copy.7 = f32[12,64,2,128]{3,2,1,0:T(2,128)} copy(f32[12,64,2,128]{3,2,1,0:T(2,128)S(1)} %bitcast.4) | data formatting | bytes 1572864

commit v3 on v2

v3 whole, which is shorter than its diff:
```python
import functools

import jax
import jax.numpy as jnp
from jax import lax
from jax.experimental import pallas as pl
from jax.experimental.pallas import tpu as pltpu
from jax.sharding import PartitionSpec as P

MESH = pl.DeviceIdType.MESH
F32, BF16 = jnp.float32, jnp.bfloat16
COLS, ROWS, HALO = 12, 64, 3
EXT = COLS + 2 * HALO
PAIRS = 2 * HALO
LINES = 2 * ROWS
TOP = LINES + PAIRS
TALL = 144
BANDS = 8
GROUPS = ((3, 6), (0, 3), (9, 3))


def stencil():
    shape = (32, 24)
    tap, term = (lax.broadcasted_iota(jnp.int32, shape, dim) for dim in range(2))
    piece, kind = term // 6, term % 6
    u, v = tap // 8 - piece // 2 - 1, tap % 8 - piece % 2 - 1
    near_u, near_v = jnp.abs(u) <= 1, jnp.abs(v) <= 1
    on_u, on_v = near_u & (v == 0), near_v & (u == 0)
    uf, vf = u.astype(F32), v.astype(F32)
    zero = jnp.zeros(shape, F32)
    centre = jnp.where((u == 0) & (v == 0), 1.0, zero)
    value = jnp.where(kind == 0, centre, zero)
    value = jnp.where((kind == 1) & on_u, 0.5 * uf, value)
    value = jnp.where((kind == 2) & on_v, 0.5 * vf, value)
    value = jnp.where((kind == 3) & on_u, 0.5 - 1.5 * centre, value)
    value = jnp.where((kind == 4) & on_v, 0.5 - 1.5 * centre, value)
    return jnp.where((kind == 5) & near_u & near_v, 0.25 * uf * vf, value)


def halves(value):
    high = value.astype(BF16)
    return high, (value - high.astype(F32)).astype(BF16)


def matrices(weights, offsets, flat, tall, mats):
    for x in range(COLS):
        w = weights[x]
        flat[:, 128 * x : 128 * x + 128] = jnp.concatenate([w[:24], w[24:]], axis=1)
    tall[...] = jnp.zeros_like(tall)
    coefs = jnp.dot(stencil(), flat[...], precision=lax.Precision.HIGHEST, preferred_element_type=F32)
    row = lax.broadcasted_iota(jnp.int32, (8, 128), 0)
    inner = lax.broadcasted_iota(jnp.int32, (8, 128), 1) % 8
    for first, count in GROUPS:
        for xl in range(count):
            x = first + xl
            o = offsets[x]
            cols = jnp.concatenate([o[0:1], o[2:3]], axis=1) + 2
            lines = jnp.concatenate([o[1:2], o[3:4]], axis=1) + 2
            shift = jnp.broadcast_to(lines, (8, 128)) + inner
            steps = jnp.broadcast_to(cols, (8, 128))
            pick = (row - shift) & 7
            in_low = row >= shift
            in_high = (row < shift) & (shift <= row + 8)
            zero = jnp.zeros((8, 128), F32)
            low, high = [], []
            for i in range(4):
                turned = jnp.take_along_axis(coefs[8 * i : 8 * i + 8, 128 * x : 128 * x + 128], pick, axis=0)
                low.append(jnp.where(in_low, turned, zero))
                high.append(jnp.where(in_high, turned, zero))
            odd, two = (steps & 1) == 1, steps >= 2
            for part, pieces in enumerate((low, high)):
                pieces = [zero] + pieces + [zero]
                once = [jnp.where(odd, pieces[d], pieces[d + 1]) for d in range(5)]
                once = [zero, zero] + once + [zero, zero]
                for d in range(7):
                    at = 16 * (xl + d) + 8 * part
                    tall[x, at : at + 8, :] = jnp.where(two, once[d], once[d + 2])
    for x in range(COLS):
        mats[:, :, 8 * x : 8 * x + 8, :] = jnp.transpose(tall[x]).reshape(2, BANDS, 8, 256)


def remap(bands, groups, field, mats, out):
    for b in bands:
        base = 16 * b if isinstance(b, int) else pl.multiple_of(16 * b, 16)
        for first, count in groups:
            depth = 16 * (count + PAIRS)
            for level in range(2):
                mat = mats[level, b, 8 * first : 8 * (first + count), :depth]
                mat_high, mat_low = halves(mat)
                cells = field[first : first + count + PAIRS, pl.ds(base + level, 16, 2), :]
                cell_high, cell_low = halves(cells.reshape(depth, 128))
                both = jnp.dot(mat_high, jnp.concatenate([cell_high, cell_low], axis=1), preferred_element_type=F32)
                result = both[:, :128] + both[:, 128:] + jnp.dot(mat_low, cell_high, preferred_element_type=F32)
                for xl in range(count):
                    out[first + xl, pl.ds(base + level, 8, 2), :] = result[8 * xl : 8 * xl + 8]


WEST, EAST, UP, DOWN, ALONG_Z, PLANE = 0, 1, 2, 5, 8, 11
LINKS = 26
ORDER = (*range(ALONG_Z, LINKS), *range(ALONG_Z))
STEPS = sorted(((j, i) for j in range(4) for i in range(4) if j + i), key=lambda s: -(s[0] % 2 + s[1] % 2 + 2 * (s[0] // 2 * (s[0] % 2 == 0) + s[1] // 2 * (s[1] % 2 == 0))))
BACK = (1, 0, 5, 7, 6, 2, 4, 3) + (10, 9, 8) + tuple(
    PLANE + STEPS.index((-j % 4, -i % 4)) for j, i in STEPS
)


def rank(gx, gy):
    return (gy >> 1) * 256 + ((gx & 15) << 3) + ((gx >> 4) << 1) + 1 - (gy & 1)


def kernel(
    owner_in, codes_in, tracers, weights_in, offsets_in, out,
    owner, codes, field, weights, offsets, flat, tall, mats, gathered, chosen, landed,
    in_sem, side_send, side_recv, row_send, row_recv, one_send, one_recv, two_send, two_recv,
    ready,
):
    gx, gy = lax.axis_index("gx"), lax.axis_index("gy")
    y, z, x = gx >> 4, (gx >> 2) & 3, gx & 3
    east, west = (gx + 1) & 63, (gx + 63) & 63
    edge = (gy == 0) | (gy == 3)
    half = COLS // 2
    edge_at = jnp.where(gy == 0, 0, LINES - PAIRS)

    loads = [
        pltpu.make_async_copy(weights_in, weights, in_sem.at[0]),
        pltpu.make_async_copy(offsets_in, offsets, in_sem.at[1]),
        pltpu.make_async_copy(owner_in, owner, in_sem.at[4]),
        pltpu.make_async_copy(codes_in, codes, in_sem.at[5]),
        pltpu.make_async_copy(tracers, field.at[HALO : HALO + COLS, PAIRS:TOP, :], in_sem.at[2]),
    ]
    own_strip = pltpu.make_async_copy(
        tracers.at[:, pl.ds(edge_at, PAIRS), :], gathered.at[z, :, 0:PAIRS, :], in_sem.at[3]
    )

    always = gy >= 0
    peers = [(west, gy), (east, gy)]
    exists = [always, always]
    for to, there in ((gy + 1, gy < 3), (gy - 1, gy > 0)):
        peers += [(gx, to), (west, to), (east, to)]
        exists += [there] * 3
    peers += [(16 * y + 4 * ((z + k) & 3) + x, gy) for k in (1, 2, 3)]
    peers += [(16 * ((y + j) & 3) + 4 * z + ((x + i) & 3), gy) for j, i in STEPS]
    exists += [edge] * 18
    mine = rank(gx, gy)
    later = [there & (rank(*to) > mine) for to, there in zip(peers, exists)]
    earlier = [there & (rank(*to) < mine) for to, there in zip(peers, exists)]

    barrier = pltpu.get_barrier_semaphore()
    for r in ORDER:

        @pl.when(later[r])
        def _():
            pl.semaphore_signal(barrier, inc=1, device_id=peers[r], device_id_type=MESH)

    @pl.when(edge)
    def _():
        own_strip.start()

    for load in loads:
        load.start()

    ahead = sum(e.astype(jnp.int32) for e in earlier)

    @pl.when(ahead > 0)
    def _():
        pl.semaphore_wait(barrier, ahead)

    def send(source, target, send_sem, recv_sem, to):
        return pltpu.make_async_remote_copy(
            src_ref=source, dst_ref=target, send_sem=send_sem, recv_sem=recv_sem, device_id=to, device_id_type=MESH
        )

    def side_copy(r):
        if r == WEST:
            source, target = tracers.at[0:HALO], field.at[HALO + COLS : EXT, PAIRS:TOP, :]
        else:
            source, target = tracers.at[COLS - HALO : COLS], field.at[0:HALO, PAIRS:TOP, :]
        return send(source, target, side_send.at[r], side_recv.at[r], peers[r])

    def row_copy(r):
        up = r < DOWN
        lines = pl.ds(LINES - PAIRS, PAIRS) if up else pl.ds(0, PAIRS)
        target = pl.ds(0, PAIRS) if up else pl.ds(TOP, PAIRS)
        which = (r - UP) % 3
        taken, put = (
            (slice(0, COLS), slice(HALO, HALO + COLS)),
            (slice(0, HALO), slice(HALO + COLS, EXT)),
            (slice(COLS - HALO, COLS), slice(0, HALO)),
        )[which]
        return send(
            tracers.at[taken, lines, :], field.at[put, target, :], row_send.at[r - UP], row_recv.at[r - UP], peers[r]
        )

    def one_copy(r):
        k = r - ALONG_Z
        return send(
            tracers.at[:, pl.ds(edge_at, PAIRS), :], gathered.at[z, :, 0:PAIRS, :], one_send.at[k], one_recv.at[z], peers[r]
        )

    def one_wait(r):
        k = r - ALONG_Z
        spot = (z + k + 1) & 3
        place = gathered.at[spot, :, 0:PAIRS, :]
        return send(place, place, one_send.at[k], one_recv.at[spot], peers[r])

    def two_copy(r):
        k = r - PLANE
        return send(
            chosen.at[k, :, 0:PAIRS, :], landed.at[y, x, :, 0:PAIRS, :], two_send.at[k], two_recv.at[y, x], peers[r]
        )

    def two_wait(r):
        k = r - PLANE
        j, i = STEPS[k]
        there = (y + j) & 3, (x + i) & 3
        return send(
            chosen.at[k, :, 0:PAIRS, :], landed.at[*there, :, 0:PAIRS, :], two_send.at[k], two_recv.at[*there], peers[r]
        )

    def copy_of(r):
        return side_copy(r) if r < UP else row_copy(r) if r < ALONG_Z else one_copy(r)

    def start_earlier(links):
        for r in links:

            @pl.when(earlier[r])
            def _():
                copy_of(r).start()

    def start_later(links, allowed):
        for r in links:

            @pl.when(later[r] & allowed(r))
            def _():
                pl.semaphore_wait(ready.at[r], 1)
                copy_of(r).start()

    wraps_west, wraps_east = (z == 0) & (x == 0), (z == 3) & (x == 3)

    def far(r):
        wrap = wraps_west if r in (WEST, UP + 1, DOWN + 1) else wraps_east if r in (EAST, UP + 2, DOWN + 2) else gy < 0
        return wrap | ((gy == 1) if UP <= r < DOWN else (gy == 2) if DOWN <= r < ALONG_Z else gy < 0)

    def near(r):
        return jnp.logical_not(far(r))

    rows, sides, plane = range(UP, ALONG_Z), (WEST, EAST), range(PLANE, LINKS)
    tower = range(ALONG_Z, PLANE)
    not_edge = jnp.logical_not(edge)

    def start_sides(who):
        for r in sides:

            @pl.when(who & earlier[r])
            def _():
                copy_of(r).start()

        start_later(sides, lambda r: who & near(r))

    start_earlier(tower)
    for r in ORDER:

        @pl.when(earlier[r])
        def _():
            pl.semaphore_signal(ready.at[BACK[r]], inc=1, device_id=peers[r], device_id_type=MESH)

    start_earlier(rows)
    start_sides(always)
    start_later(rows, near)
    start_later(tower, lambda r: always)

    for c in range(EXT):
        field[c, TOP + PAIRS : TALL, :] = jnp.zeros((TALL - TOP - PAIRS, 128), F32)

    loads[0].wait()
    loads[1].wait()
    matrices(weights, offsets, flat, tall, mats)
    for load in loads[2:]:
        load.wait()

    side = jnp.where(gy == 0, 0, 1)

    @pl.when(edge)
    def _():
        own_strip.wait()
        for r in tower:
            one_wait(r).wait_recv()
        for r in (*plane, None):
            target = gx if r is None else peers[r][0]
            block = owner[side, target]
            parts = [
                gathered[(from_block >> 2) & 3, cols, 0:PAIRS, :]
                for from_block, cols in (
                    ((block + 63) & 63, slice(COLS - HALO, COLS)),
                    (block, slice(0, COLS)),
                    ((block + 1) & 63, slice(0, HALO)),
                )
            ]
            for part, cols in zip(parts, (slice(0, HALO), slice(HALO, HALO + COLS), slice(HALO + COLS, EXT))):
                if r is None:
                    landed[y, x, cols, 0:PAIRS, :] = part
                else:
                    chosen[r - PLANE, cols, 0:PAIRS, :] = part
            if r is not None:

                @pl.when(later[r])
                def _():
                    pl.semaphore_wait(ready.at[r], 1)

                two_copy(r).start()

    remap((1, 2, 3, 4, 5, 6), GROUPS[:1], field, mats, out)

    start_later(rows, far)
    start_later(sides, far)

    for r in sides:
        side_copy(r).wait()
    remap((1, 2, 3, 4, 5, 6), GROUPS[1:], field, mats, out)

    @pl.when(gy > 0)
    def _():
        for r in range(UP, DOWN):
            row_copy(r).wait_recv()
        remap((0,), GROUPS, field, mats, out)

    @pl.when(gy < 3)
    def _():
        for r in range(DOWN, ALONG_Z):
            row_copy(r).wait_recv()
        remap((7,), GROUPS, field, mats, out)

    @pl.when(edge)
    def _():
        for r in plane:
            two_wait(r).wait_recv()
        block = owner[side, gx]
        code = codes[side, gx]
        turn, flip = code & 1, (code >> 1) & 1
        before, after = (block + 63) & 63, (block + 1) & 63
        first, last = jnp.where(turn == 1, after, before), jnp.where(turn == 1, before, after)
        for u in range(EXT):
            v = jnp.where(turn == 1, EXT - 1 - u, u)
            part = first if u < HALO else block if u < HALO + COLS else last
            piece = landed[part >> 4, part & 3, v, 0:PAIRS, :]
            back = jnp.concatenate([piece[4:6], piece[2:4], piece[0:2]], axis=0)
            piece = jnp.where(flip == 1, back, piece)

            @pl.when(gy == 0)
            def _():
                field[u, 0:PAIRS, :] = piece

            @pl.when(gy == 3)
            def _():
                field[u, TOP : TOP + PAIRS, :] = piece

        remap((jnp.where(gy == 0, 0, BANDS - 1),), GROUPS, field, mats, out)
        for r in tower:
            one_copy(r).wait_send()
        for r in plane:
            two_copy(r).wait_send()

    @pl.when(gy < 3)
    def _():
        for r in range(UP, DOWN):
            row_copy(r).wait_send()

    @pl.when(gy > 0)
    def _():
        for r in range(DOWN, ALONG_Z):
            row_copy(r).wait_send()


def on_device(tracers, weights, offsets, owner, codes):
    lines = tracers.reshape(COLS, LINES, 128)
    hbm = pl.BlockSpec(memory_space=pltpu.HBM)
    vmem = pl.BlockSpec(memory_space=pltpu.VMEM)
    dma = pltpu.SemaphoreType.DMA
    result = pl.pallas_call(
        kernel,
        out_shape=jax.ShapeDtypeStruct((COLS, LINES, 128), F32),
        in_specs=[hbm] * 5,
        out_specs=vmem,
        scratch_shapes=[
            pltpu.SMEM((2, 64), jnp.int32),
            pltpu.SMEM((2, 64), jnp.int32),
            pltpu.VMEM((EXT, TALL, 128), F32),
            pltpu.VMEM((COLS, 48, ROWS), F32),
            pltpu.VMEM((COLS, 4, ROWS), jnp.int32),
            pltpu.VMEM((24, 128 * COLS), F32),
            pltpu.VMEM((COLS, 256, 128), F32),
            pltpu.VMEM((2, BANDS, 8 * COLS, 256), F32),
            pltpu.VMEM((4, COLS, 8, 128), F32),
            pltpu.VMEM((15, EXT, 8, 128), F32),
            pltpu.VMEM((4, 4, EXT, 8, 128), F32),
            dma((6,)), dma((2,)), dma((2,)), dma((6,)), dma((6,)), dma((3,)), dma((4,)), dma((15,)), dma((4, 4)), pltpu.SemaphoreType.REGULAR((LINKS,)),
        ],
        compiler_params=pltpu.CompilerParams(
            collective_id=0, has_side_effects=True, vmem_limit_bytes=40 * 1024 * 1024
        ),
    )(*(pltpu.with_memory_space_constraint(a, pltpu.HBM) for a in (owner, codes, lines, jnp.transpose(weights, (0, 2, 1)), jnp.transpose(offsets, (0, 2, 1)))))
    return result.reshape(COLS, ROWS, 2, 128)


def solution(mesh):
    in_specs = (P("gx", "gy", None, None), P("gx", "gy", None), P("gx", "gy", None), P(), P())
    return jax.shard_map(
        on_device, mesh=mesh, in_specs=in_specs, out_specs=P("gx", "gy", None, None), check_vma=False
    )
```

time: 25 us -> 23.5 us (0.940)
  the two profiles are of different devices: /device:TPU:6 before, /device:TPU:36 now
where the time goes in v3:
time: 23.5 us; the launch traced here: 23.4 us
  Pallas kernels  22.5 us (96%)
  local copies, waits for them, and re-layouts  0.88 us (4%)
    pallas_call x1, Pallas kernels, on_device(): pl.pallas_call(kernel, out_shape=jax.ShapeDtypeStruct((COLS, LINES, 128),...  22.5 us
    unnamed x1, local copies, waits for them, and re-layouts  0.88 us

profile of v3, /device:TPU:36, one launch (start us, length us, event | category | flops | bytes accessed | tf_op | source)
XLA Modules:
  0.0 23.4 jit_solution(409100615193594880)
XLA Ops:
  0.0 22.5 %shard_map.55 = f32[12,128,128]{2,1,0:T(8,128)S(1)} custom-call(s32[2,64]{1,0:T(2,128)} %owner_in.1, s32[2,64]{1,0:T(2,128)} %codes_in.1, f32[12,128,128]{2,1,0:T(8,128)} %bitcast.5, f32[12,48,64]{2,1,0:T(8,128)} %bitcast.6, s32[12,4,64]{2,1,0:T(4,128)} %bitcast.7), custom_call_target="tpu_custom_call" | custom-call | tf_op jit(solution)/shard_map/pallas_call | solution.py:379
  22.5 0.9 %copy.7 = f32[12,64,2,128]{3,2,1,0:T(2,128)} copy(f32[12,64,2,128]{3,2,1,0:T(2,128)S(1)} %bitcast.4) | data formatting | bytes 1572864

commit v4 on v3

--- a/solution.py
+++ b/solution.py
@@ -96,12 +96,12 @@
 
 
 WEST, EAST, UP, DOWN, ALONG_Z, PLANE = 0, 1, 2, 5, 8, 11
-LINKS = 26
+VIA, LINKS = 26, 27
 ORDER = (*range(ALONG_Z, LINKS), *range(ALONG_Z))
 STEPS = sorted(((j, i) for j in range(4) for i in range(4) if j + i), key=lambda s: -(s[0] % 2 + s[1] % 2 + 2 * (s[0] // 2 * (s[0] % 2 == 0) + s[1] // 2 * (s[1] % 2 == 0))))
 BACK = (1, 0, 5, 7, 6, 2, 4, 3) + (10, 9, 8) + tuple(
     PLANE + STEPS.index((-j % 4, -i % 4)) for j, i in STEPS
-)
+) + (VIA,)
 
 
 def rank(gx, gy):
@@ -110,9 +110,9 @@
 
 def kernel(
     owner_in, codes_in, tracers, weights_in, offsets_in, out,
-    owner, codes, field, weights, offsets, flat, tall, mats, gathered, chosen, landed,
+    owner, codes, field, weights, offsets, flat, tall, mats, gathered, chosen, landed, relay,
     in_sem, side_send, side_recv, row_send, row_recv, one_send, one_recv, two_send, two_recv,
-    ready,
+    via_send, via_recv, hand_send, ready,
 ):
     gx, gy = lax.axis_index("gx"), lax.axis_index("gy")
     y, z, x = gx >> 4, (gx >> 2) & 3, gx & 3
@@ -141,6 +141,17 @@
     peers += [(16 * y + 4 * ((z + k) & 3) + x, gy) for k in (1, 2, 3)]
     peers += [(16 * ((y + j) & 3) + 4 * z + ((x + i) & 3), gy) for j, i in STEPS]
     exists += [edge] * 18
+    wraps_west, wraps_east = (z == 0) & (x == 0), (z == 3) & (x == 3)
+    hands_west, hands_east = edge & (z == 0) & (x == 1), edge & (z == 3) & (x == 2)
+    via_to_east, via_to_west = edge & wraps_east, edge & wraps_west
+    up_y, down_y = 16 * ((y + 1) & 3), 16 * ((y + 3) & 3)
+    via = jnp.where(
+        via_to_east, up_y + 1, jnp.where(hands_west, down_y + 15, jnp.where(via_to_west, down_y + 14, up_y))
+    )
+    peers += [(via, gy)]
+    exists += [via_to_east | via_to_west | hands_west | hands_east]
+    exists[WEST] = jnp.logical_not(via_to_west)
+    exists[EAST] = jnp.logical_not(via_to_east)
     mine = rank(gx, gy)
     later = [there & (rank(*to) > mine) for to, there in zip(peers, exists)]
     earlier = [there & (rank(*to) < mine) for to, there in zip(peers, exists)]
@@ -235,8 +246,6 @@
                 pl.semaphore_wait(ready.at[r], 1)
                 copy_of(r).start()
 
-    wraps_west, wraps_east = (z == 0) & (x == 0), (z == 3) & (x == 3)
-
     def far(r):
         wrap = wraps_west if r in (WEST, UP + 1, DOWN + 1) else wraps_east if r in (EAST, UP + 2, DOWN + 2) else gy < 0
         return wrap | ((gy == 1) if UP <= r < DOWN else (gy == 2) if DOWN <= r < ALONG_Z else gy < 0)
@@ -244,7 +253,37 @@
     def near(r):
         return jnp.logical_not(far(r))
 
-    rows, sides, plane = range(UP, ALONG_Z), (WEST, EAST), range(PLANE, LINKS)
+    def via_copy(r, c, column):
+        return send(tracers.at[column], relay.at[c], via_send.at[c], via_recv.at[c], peers[r])
+
+    def start_via(allowed, r, first):
+        @pl.when(allowed)
+        def _():
+            for c in range(HALO):
+                via_copy(r, c, first + c).start()
+
+    def hand_copy(r, c):
+        column = c if r == EAST else HALO + COLS + c
+        return send(relay.at[c], field.at[column, PAIRS:TOP, :], hand_send.at[c], side_recv.at[r], peers[VIA])
+
+    def hand_on(allowed, r):
+        @pl.when(allowed & later[VIA])
+        def _():
+            pl.semaphore_wait(ready.at[VIA], 1)
+
+        @pl.when(allowed)
+        def _():
+            for c in range(HALO):
+                via_copy(r, c, c).wait_recv()
+                hand_copy(r, c).start()
+
+    def hand_wait(allowed, r):
+        @pl.when(allowed)
+        def _():
+            for c in range(HALO):
+                hand_copy(r, c).wait_send()
+
+    rows, sides, plane = range(UP, ALONG_Z), (WEST, EAST), range(PLANE, VIA)
     tower = range(ALONG_Z, PLANE)
     not_edge = jnp.logical_not(edge)
 
@@ -265,9 +304,13 @@
             pl.semaphore_signal(ready.at[BACK[r]], inc=1, device_id=peers[r], device_id_type=MESH)
 
     start_earlier(rows)
-    start_sides(always)
-    start_later(rows, near)
+    start_sides(not_edge)
+    start_via(via_to_east, WEST, COLS - HALO)
+    start_later(rows, lambda r: near(r) & not_edge)
     start_later(tower, lambda r: always)
+    start_sides(edge)
+    start_via(via_to_west, EAST, 0)
+    start_later(rows, lambda r: near(r) & edge)
 
     for c in range(EXT):
         field[c, TOP + PAIRS : TALL, :] = jnp.zeros((TALL - TOP - PAIRS, 128), F32)
@@ -279,6 +322,8 @@
         load.wait()
 
     side = jnp.where(gy == 0, 0, 1)
+
+    hand_on(hands_east, EAST)
 
     @pl.when(edge)
     def _():
@@ -288,19 +333,14 @@
         for r in (*plane, None):
             target = gx if r is None else peers[r][0]
             block = owner[side, target]
-            parts = [
-                gathered[(from_block >> 2) & 3, cols, 0:PAIRS, :]
-                for from_block, cols in (
-                    ((block + 63) & 63, slice(COLS - HALO, COLS)),
-                    (block, slice(0, COLS)),
-                    ((block + 1) & 63, slice(0, HALO)),
-                )
-            ]
-            for part, cols in zip(parts, (slice(0, HALO), slice(HALO, HALO + COLS), slice(HALO + COLS, EXT))):
-                if r is None:
-                    landed[y, x, cols, 0:PAIRS, :] = part
-                else:
-                    chosen[r - PLANE, cols, 0:PAIRS, :] = part
+            before, after = (block + 63) & 63, (block + 1) & 63
+            column = gx & 51
+            pick = jnp.where((before & 51) == column, before, jnp.where((after & 51) == column, after, block))
+            part = gathered[(pick >> 2) & 3, :, 0:PAIRS, :]
+            if r is None:
+                landed[y, x, :, 0:PAIRS, :] = part
+            else:
+                chosen[r - PLANE, :, 0:PAIRS, :] = part
             if r is not None:
 
                 @pl.when(later[r])
@@ -311,11 +351,12 @@
 
     remap((1, 2, 3, 4, 5, 6), GROUPS[:1], field, mats, out)
 
+    hand_on(hands_west, WEST)
+    start_later(sides, far)
     start_later(rows, far)
-    start_later(sides, far)
 
     for r in sides:
-        side_copy(r).wait()
+        side_copy(r).wait_recv()
     remap((1, 2, 3, 4, 5, 6), GROUPS[1:], field, mats, out)
 
     @pl.when(gy > 0)
@@ -340,8 +381,12 @@
         before, after = (block + 63) & 63, (block + 1) & 63
         first, last = jnp.where(turn == 1, after, before), jnp.where(turn == 1, before, after)
         for u in range(EXT):
-            v = jnp.where(turn == 1, EXT - 1 - u, u)
-            part = first if u < HALO else block if u < HALO + COLS else last
+            if u < HALO:
+                part, v = first, jnp.where(turn == 1, HALO - 1 - u, COLS - HALO + u)
+            elif u < HALO + COLS:
+                part, v = block, jnp.where(turn == 1, EXT - HALO - 1 - u, u - HALO)
+            else:
+                part, v = last, jnp.where(turn == 1, COLS - HALO + EXT - 1 - u, u - HALO - COLS)
             piece = landed[part >> 4, part & 3, v, 0:PAIRS, :]
             back = jnp.concatenate([piece[4:6], piece[2:4], piece[0:2]], axis=0)
             piece = jnp.where(flip == 1, back, piece)
@@ -359,6 +404,24 @@
             one_copy(r).wait_send()
         for r in plane:
             two_copy(r).wait_send()
+
+    for r, skip in ((WEST, via_to_west), (EAST, via_to_east)):
+
+        @pl.when(jnp.logical_not(skip))
+        def _():
+            side_copy(r).wait_send()
+
+    @pl.when(via_to_west | via_to_east)
+    def _():
+        for c in range(HALO):
+            via_copy(WEST, c, c).wait_send()
+
+    @pl.when(via_to_west & later[VIA])
+    def _():
+        pl.semaphore_wait(ready.at[VIA], 1)
+
+    hand_wait(hands_west, WEST)
+    hand_wait(hands_east, EAST)
 
     @pl.when(gy < 3)
     def _():
@@ -391,9 +454,10 @@
             pltpu.VMEM((COLS, 256, 128), F32),
             pltpu.VMEM((2, BANDS, 8 * COLS, 256), F32),
             pltpu.VMEM((4, COLS, 8, 128), F32),
-            pltpu.VMEM((15, EXT, 8, 128), F32),
-            pltpu.VMEM((4, 4, EXT, 8, 128), F32),
-            dma((6,)), dma((2,)), dma((2,)), dma((6,)), dma((6,)), dma((3,)), dma((4,)), dma((15,)), dma((4, 4)), pltpu.SemaphoreType.REGULAR((LINKS,)),
+            pltpu.VMEM((15, COLS, 8, 128), F32),
+            pltpu.VMEM((4, 4, COLS, 8, 128), F32),
+            pltpu.VMEM((HALO, LINES, 128), F32),
+            dma((6,)), dma((2,)), dma((2,)), dma((6,)), dma((6,)), dma((3,)), dma((4,)), dma((15,)), dma((4, 4)), dma((3,)), dma((3,)), dma((3,)), pltpu.SemaphoreType.REGULAR((LINKS,)),
         ],
         compiler_params=pltpu.CompilerParams(
             collective_id=0, has_side_effects=True, vmem_limit_bytes=40 * 1024 * 1024

time: 23.5 us -> 21.9 us (0.932)
  the two profiles are of different devices: /device:TPU:36 before, /device:TPU:8 now
where the time goes in v4:
time: 21.9 us; the launch traced here: 21.8 us
  Pallas kernels  20.9 us (95%)
  local copies, waits for them, and re-layouts  0.88 us (4%)
    pallas_call x1, Pallas kernels, on_device(): pl.pallas_call(kernel, out_shape=jax.ShapeDtypeStruct((COLS, LINES, 128),...  20.9 us
    unnamed x1, local copies, waits for them, and re-layouts  0.88 us

profile of v4, /device:TPU:8, one launch (start us, length us, event | category | flops | bytes accessed | tf_op | source)
XLA Modules:
  0.0 21.8 jit_solution(5319860494706009143)
XLA Ops:
  0.0 20.9 %shard_map.55 = f32[12,128,128]{2,1,0:T(8,128)S(1)} custom-call(s32[2,64]{1,0:T(2,128)} %owner_in.1, s32[2,64]{1,0:T(2,128)} %codes_in.1, f32[12,128,128]{2,1,0:T(8,128)} %bitcast.5, f32[12,48,64]{2,1,0:T(8,128)} %bitcast.6, s32[12,4,64]{2,1,0:T(4,128)} %bitcast.7), custom_call_target="tpu_custom_call" | custom-call | tf_op jit(solution)/shard_map/pallas_call | solution.py:442
  21.0 0.9 %copy.7 = f32[12,64,2,128]{3,2,1,0:T(2,128)} copy(f32[12,64,2,128]{3,2,1,0:T(2,128)S(1)} %bitcast.4) | data formatting | bytes 1572864

commit v5 on v4

--- a/solution.py
+++ b/solution.py
@@ -288,13 +288,14 @@
     not_edge = jnp.logical_not(edge)
 
     def start_sides(who):
+        start_later((EAST,), lambda r: who & near(r) & (x == 3))
         for r in sides:
 
             @pl.when(who & earlier[r])
             def _():
                 copy_of(r).start()
 
-        start_later(sides, lambda r: who & near(r))
+        start_later(sides, lambda r: who & near(r) & ((x < 3) if r == EAST else always))
 
     start_earlier(tower)
     for r in ORDER:

time: 21.9 us -> 21.9 us (level)
  no operation moved by 1% of the time
where the time goes in v5:
time: 21.9 us; the launch traced here: 21.8 us
  Pallas kernels  21 us (96%)
  local copies, waits for them, and re-layouts  0.88 us (4%)
    pallas_call x1, Pallas kernels, on_device(): pl.pallas_call(kernel, out_shape=jax.ShapeDtypeStruct((COLS, LINES, 128),...  21 us
    unnamed x1, local copies, waits for them, and re-layouts  0.88 us

profile of v5, /device:TPU:8, one launch (start us, length us, event | category | flops | bytes accessed | tf_op | source)
XLA Modules:
  0.0 21.8 jit_solution(356424919297837602)
XLA Ops:
  0.0 21.0 %shard_map.55 = f32[12,128,128]{2,1,0:T(8,128)S(1)} custom-call(s32[2,64]{1,0:T(2,128)} %owner_in.1, s32[2,64]{1,0:T(2,128)} %codes_in.1, f32[12,128,128]{2,1,0:T(8,128)} %bitcast.5, f32[12,48,64]{2,1,0:T(8,128)} %bitcast.6, s32[12,4,64]{2,1,0:T(4,128)} %bitcast.7), custom_call_target="tpu_custom_call" | custom-call | tf_op jit(solution)/shard_map/pallas_call | solution.py:443
  21.0 0.9 %copy.7 = f32[12,64,2,128]{3,2,1,0:T(2,128)} copy(f32[12,64,2,128]{3,2,1,0:T(2,128)S(1)} %bitcast.4) | data formatting | bytes 1572864

commit v6 on v4

--- a/solution.py
+++ b/solution.py
@@ -98,7 +98,7 @@
 WEST, EAST, UP, DOWN, ALONG_Z, PLANE = 0, 1, 2, 5, 8, 11
 VIA, LINKS = 26, 27
 ORDER = (*range(ALONG_Z, LINKS), *range(ALONG_Z))
-STEPS = sorted(((j, i) for j in range(4) for i in range(4) if j + i), key=lambda s: -(s[0] % 2 + s[1] % 2 + 2 * (s[0] // 2 * (s[0] % 2 == 0) + s[1] // 2 * (s[1] % 2 == 0))))
+STEPS = sorted(((j, i) for j in range(4) for i in range(4) if j + i), key=lambda s: (-(0, 1, 2, 1)[s[1]], -(0, 1, 2, 1)[s[0]]))
 BACK = (1, 0, 5, 7, 6, 2, 4, 3) + (10, 9, 8) + tuple(
     PLANE + STEPS.index((-j % 4, -i % 4)) for j, i in STEPS
 ) + (VIA,)

time: 21.9 us -> 21.9 us (level)
  no operation moved by 1% of the time
where the time goes in v6:
time: 21.9 us; the launch traced here: 21.8 us
  Pallas kernels  20.9 us (95%)
  local copies, waits for them, and re-layouts  0.88 us (4%)
    pallas_call x1, Pallas kernels, on_device(): pl.pallas_call(kernel, out_shape=jax.ShapeDtypeStruct((COLS, LINES, 128),...  20.9 us
    unnamed x1, local copies, waits for them, and re-layouts  0.88 us

profile of v6, /device:TPU:8, one launch (start us, length us, event | category | flops | bytes accessed | tf_op | source)
XLA Modules:
  0.0 21.8 jit_solution(17560643475153562484)
XLA Ops:
  0.0 20.9 %shard_map.55 = f32[12,128,128]{2,1,0:T(8,128)S(1)} custom-call(s32[2,64]{1,0:T(2,128)} %owner_in.1, s32[2,64]{1,0:T(2,128)} %codes_in.1, f32[12,128,128]{2,1,0:T(8,128)} %bitcast.5, f32[12,48,64]{2,1,0:T(8,128)} %bitcast.6, s32[12,4,64]{2,1,0:T(4,128)} %bitcast.7), custom_call_target="tpu_custom_call" | custom-call | tf_op jit(solution)/shard_map/pallas_call | solution.py:442
  20.9 0.9 %copy.7 = f32[12,64,2,128]{3,2,1,0:T(2,128)} copy(f32[12,64,2,128]{3,2,1,0:T(2,128)S(1)} %bitcast.4) | data formatting | bytes 1572864
